TPU v7x, 512 devices: a whole 4x8x8 slice. The times are simulated.
512 devices in a mesh: agents: 64 (over y_lo, z, core), heads: 8 (over x, y_hi).
Axes of the slice: x: 4, y: 8 (y_hi: 2, y_lo: 4; y = y_hi * 4 + y_lo), z: 8, core: 2. Of those that a mesh axis runs over, the one named last changes fastest.
Arguments:
- queries: bfloat16 [128, 8192], P('agents', 'heads'), as said below
- global_kv: bfloat16 [2, 32768, 1024], P(None, 'agents', 'heads'), as said below
- team_kv: bfloat16 [2, 131072, 1024], P(None, 'agents', 'heads'), may hold values from -8 to 8
- suffix_kv: bfloat16 [2, 128, 128, 1024], P(None, 'agents', None, 'heads'), may hold values from -10 to 10
- team_lengths: int32 [64], replicated, may hold values from 128 to 2048, as said below
- team_map: int32 [128], replicated, may hold values from 0 to 63, as said below
- suffix_lengths: int32 [128], P('agents'), may hold values from 1 to 128, as said below
- team_owner: int32 [64], replicated, may hold values from 0 to 63, each once
- out_weight: bfloat16 [8192, 8192], P('heads', 'agents'), may hold values from -0.0625 to 0.0625
Outputs:
- layer_out: bfloat16 [128, 8192], P('heads', 'agents')
Inputs may be any that keep to these rules, and one draw needn't show every extreme that they name: `queries`: entries of order one; a few agents may have much larger entries. `global_kv`: entries of order one. `team_lengths`: every team prompt has at most 2048 tokens and some team has exactly 2048. `team_map`: no team has more than 8 agents and some team has exactly 8. `suffix_lengths`: every suffix has at most 128 tokens and some agent has exactly 128. `team_owner`: each index of agents owns exactly one team.
All inputs are finite; a program needn't handle non-finite values.
Results may differ from a plain program's by a relative error of at most 0.017.
Values may be sent and summed in bfloat16 or wider, within the bound.
A program may use at most 192 MiB of HBM per device.

v0:
```python
import math

import jax
import jax.numpy as jnp
from jax import lax
from jax.sharding import PartitionSpec as P

HEAD_DIM = 128
TEAM_CAP = 8


NEG = -1e30


def key_partial(query_block, key_block, value_block, allowed, scaling):
    scores = (
        jnp.einsum("ajgd,tjd->ajgt", query_block, key_block, preferred_element_type=jnp.float32)
        * scaling
    )
    scores = jnp.where(allowed, scores, NEG)
    highest = jnp.max(scores, axis=-1)
    weights = jnp.where(allowed, jnp.exp(scores - highest[..., None]), 0.0)
    weight_sum = jnp.sum(weights, axis=-1)
    numerator = jnp.einsum(
        "ajgt,tjd->ajgd",
        weights.astype(jnp.bfloat16),
        value_block,
        preferred_element_type=jnp.float32,
    )
    return (numerator, highest, weight_sum)


def combine_parts(first_part, second_part):
    first_num, first_high, first_mass = first_part
    second_num, second_high, second_mass = second_part
    highest = jnp.maximum(first_high, second_high)
    first_factor = jnp.exp(first_high - highest)
    second_factor = jnp.exp(second_high - highest)
    numerator = first_num * first_factor[..., None] + second_num * second_factor[..., None]
    return (numerator, highest, first_mass * first_factor + second_mass * second_factor)


def team_partial(query_rows, team_map, team_slab, team_id, length, offset, scaling):
    agents_total = query_rows.shape[0]
    kv_heads = query_rows.shape[1]
    group_size = query_rows.shape[2]
    positions = jnp.arange(agents_total, dtype=jnp.int32)
    is_member = team_map == team_id
    ordering = jnp.where(is_member, positions, positions + agents_total)
    members = jnp.argsort(ordering)[:TEAM_CAP]
    is_live = is_member[members]
    member_rows = query_rows[members]
    span = team_slab.shape[1]
    block_size = math.gcd(span, 512)
    used_blocks = jnp.clip((length - offset + block_size - 1) // block_size, 0, span // block_size)
    initial = (
        jnp.zeros((TEAM_CAP, kv_heads, group_size, HEAD_DIM), jnp.float32),
        jnp.full((TEAM_CAP, kv_heads, group_size), NEG, jnp.float32),
        jnp.zeros((TEAM_CAP, kv_heads, group_size), jnp.float32),
    )

    def add_block(block_index, carried):
        first_key = block_index * block_size
        key_block = lax.dynamic_slice_in_dim(team_slab[0], first_key, block_size, 0).reshape(
            block_size, kv_heads, HEAD_DIM
        )
        value_block = lax.dynamic_slice_in_dim(team_slab[1], first_key, block_size, 0).reshape(
            block_size, kv_heads, HEAD_DIM
        )
        allowed = offset + first_key + jnp.arange(block_size, dtype=jnp.int32) < length
        fresh = key_partial(member_rows, key_block, value_block, allowed, scaling)
        return combine_parts(carried, fresh)

    result = lax.fori_loop(0, used_blocks, add_block, initial)
    target = jnp.where(is_live, members, agents_total)
    return (result, target)


def fold_rows(partial_rows, extra, target):
    numerator, highest, weight_sum = partial_rows
    safe_rows = jnp.minimum(target, numerator.shape[0] - 1)
    picked = (numerator[safe_rows], highest[safe_rows], weight_sum[safe_rows])
    merged = combine_parts(picked, extra)
    return (
        numerator.at[target].set(merged[0], mode="drop"),
        highest.at[target].set(merged[1], mode="drop"),
        weight_sum.at[target].set(merged[2], mode="drop"),
    )


def suffix_partial(own_rows, suffix_kv, suffix_lengths, scaling):
    agent_dev = own_rows.shape[0]
    kv_heads = own_rows.shape[1]
    suffix_keys = suffix_kv[0].reshape(agent_dev, -1, kv_heads, HEAD_DIM)
    suffix_values = suffix_kv[1].reshape(agent_dev, -1, kv_heads, HEAD_DIM)
    slots = jnp.arange(suffix_keys.shape[1], dtype=jnp.int32)
    allowed = (slots[None, :] < suffix_lengths[:, None])[:, None, None, :]
    scores = (
        jnp.einsum("ajgd,asjd->ajgs", own_rows, suffix_keys, preferred_element_type=jnp.float32)
        * scaling
    )
    scores = jnp.where(allowed, scores, NEG)
    highest = jnp.max(scores, axis=-1)
    weights = jnp.where(allowed, jnp.exp(scores - highest[..., None]), 0.0)
    numerator = jnp.einsum(
        "ajgs,asjd->ajgd",
        weights.astype(jnp.bfloat16),
        suffix_values,
        preferred_element_type=jnp.float32,
    )
    return (numerator, highest, jnp.sum(weights, axis=-1))


def shards(
    queries,
    global_kv,
    team_kv,
    suffix_kv,
    team_lengths,
    team_map,
    suffix_lengths,
    team_owner,
    out_weight,
):
    agent_dev = queries.shape[0]
    kv_width = global_kv.shape[2]
    kv_heads = kv_width // HEAD_DIM
    group_size = queries.shape[1] // kv_width
    scaling = 1.0 / math.sqrt(HEAD_DIM)
    agent_devices = lax.axis_size("agents")
    position = lax.axis_index("agents")
    gathered = lax.all_gather(queries, "agents", axis=0, tiled=True)
    agents_total = gathered.shape[0]
    query_rows = gathered.reshape(agents_total, kv_heads, group_size, HEAD_DIM)
    glob_keys = global_kv[0].reshape(-1, kv_heads, HEAD_DIM)
    glob_values = global_kv[1].reshape(-1, kv_heads, HEAD_DIM)
    block_agents = math.gcd(agents_total, max(1, 512 // (kv_heads * group_size)))
    query_blocks = query_rows.reshape(
        agents_total // block_agents, block_agents, kv_heads, group_size, HEAD_DIM
    )

    def global_block(query_block):
        return key_partial(query_block, glob_keys, glob_values, True, scaling)

    numerator, highest, weight_sum = lax.map(global_block, query_blocks)
    partial_rows = (
        numerator.reshape(agents_total, kv_heads, group_size, HEAD_DIM),
        highest.reshape(agents_total, kv_heads, group_size),
        weight_sum.reshape(agents_total, kv_heads, group_size),
    )
    team_ids = jnp.arange(team_owner.shape[0], dtype=jnp.int32)
    own_team = jnp.sum(jnp.where(team_owner == position, team_ids, 0))
    team_result, team_target = team_partial(
        query_rows, team_map, team_kv, own_team, team_lengths[own_team], 0, scaling
    )
    partial_rows = fold_rows(partial_rows, team_result, team_target)
    own_rows = queries.reshape(agent_dev, kv_heads, group_size, HEAD_DIM)
    suffix_parts = suffix_partial(own_rows, suffix_kv, suffix_lengths, scaling)
    outgoing = (
        partial_rows[0].reshape(agent_devices, agent_dev, kv_heads, group_size, HEAD_DIM),
        partial_rows[1].reshape(agent_devices, agent_dev, kv_heads, group_size),
        partial_rows[2].reshape(agent_devices, agent_dev, kv_heads, group_size),
    )
    got_num, got_high, got_mass = (
        lax.all_to_all(outgoing[0], "agents", split_axis=0, concat_axis=0, tiled=True),
        lax.all_to_all(outgoing[1], "agents", split_axis=0, concat_axis=0, tiled=True),
        lax.all_to_all(outgoing[2], "agents", split_axis=0, concat_axis=0, tiled=True),
    )
    overall = jnp.maximum(jnp.max(got_high, axis=0), suffix_parts[1])
    factors = jnp.exp(got_high - overall[None])
    suffix_factor = jnp.exp(suffix_parts[1] - overall)
    numer_total = (
        jnp.sum(got_num * factors[..., None], axis=0) + suffix_parts[0] * suffix_factor[..., None]
    )
    mass_total = jnp.sum(got_mass * factors, axis=0) + suffix_parts[2] * suffix_factor
    attention = (numer_total / mass_total[..., None]).reshape(agent_dev, -1).astype(jnp.bfloat16)
    projected = jnp.dot(
        lax.all_gather(attention, "agents", axis=0, tiled=True),
        out_weight,
        preferred_element_type=jnp.float32,
    )
    summed = lax.psum_scatter(
        projected.astype(jnp.bfloat16), "heads", scatter_dimension=0, tiled=True
    )
    return summed


def solution(mesh):
    return jax.shard_map(
        shards,
        mesh=mesh,
        in_specs=(
            P("agents", "heads"),
            P(None, "agents", "heads"),
            P(None, "agents", "heads"),
            P(None, "agents", None, "heads"),
            P(),
            P(),
            P("agents"),
            P(),
            P("heads", "agents"),
        ),
        out_specs=P("heads", "agents"),
        check_vma=False,
    )
```

profile of v0, /device:TPU:1, one launch (start us, length us, event | category | flops | bytes accessed | tf_op | source)
XLA Modules:
  0.0 328.7 jit_solution(14783468035776591276)
XLA Ops:
  6.5 1.4 fusion.67
  9.9 1.3 dynamic_slice.13
  11.7 88.0 %all-gather = bf16[64,2,1024]{2,1,0:T(2,128)(2,1)S(1)} all-gather(bf16[1,2,1024]{2,1,0:T(2,128)(2,1)} %bitcast.207), channel_id=1, replica_groups=mesh['agents'=64,'heads'=8] {'agents'}, dimensions={0}, use_global_device_ids=true | all-gather | bytes 266240 | tf_op jit(solution)/shard_map/all_gather | solution.py:132
  100.1 0.6 copy-done.5
  101.4 2.6 sort.17
  104.6 2.9 while.29
  107.5 0.6 gather_fusion
  108.5 4.7 %while.28 = (s32[]{:T(128)}, f32[2,64,1,8,128]{4,3,1,2,0:T(8,128)}, f32[2,64,1,8]{3,1,2,0:T(8,128)}, f32[2,64,1,8]{3,1,2,0:T(8,128)}, bf16[2,64,1,8,128]{4,3,1,2...) while((s32[]{:T(128)}, f32[2,64,1,8,128]{4,3,1,2,0:T(8,128)}, ...), condition=%wide.region_3.4_spmd, body=%wide.region_0.3_spmd.sunk | while | flops 135789568 | bytes 3880025 | solution.py:145
  109.8 1.0 fusion.92
  112.2 1.1 fusion.92
  113.3 1.4 gather_fusion.2
  114.7 2.0 scatter_custom_fusion.1
  116.7 7.1 %all-to-all-start.1 = ((f32[64,2,1,8]{3,1,2,0:T(2,128)}), f32[64,2,1,8]{3,1,2,0:T(2,128)S(1)}, u32[]{:S(2)}, u32[]{:S(2)}) async-start(f32[64,2,1,8]{3,1,2,0:T(2,128)} %bitcast.47), calls=%async_computation.1 | async-start | bytes 131072 | tf_op jit(solution)/shard_map/all_to_all | solution.py:166
  123.8 1.6 gather_fusion.1
  125.4 3.0 scatter_custom_fusion.2
  128.4 5.4 %all-to-all-done.1 = f32[64,2,1,8]{3,1,2,0:T(2,128)S(1)} async-done(((f32[64,2,1,8]{3,1,2,0:T(2,128)}), f32[64,2,1,8]{3,1,2,0:T(2,128)S(1)}, u32[]{:S(2)}, u32[]{:S(2)}) %all-to-all-start.1) | async-done | bytes 4128 | tf_op jit(solution)/shard_map/all_to_all | solution.py:166
  133.8 5.3 %all-to-all-start.2 = ((f32[64,2,1,8]{3,1,2,0:T(2,128)}), f32[64,2,1,8]{3,1,2,0:T(2,128)S(1)}, u32[]{:S(2)}, u32[]{:S(2)}) async-start(f32[64,2,1,8]{3,1,2,0:T(2,128)} %bitcast.55), calls=%async_computation.2 | async-start | bytes 131072 | tf_op jit(solution)/shard_map/all_to_all | solution.py:167
  139.2 1.5 scatter_fusion
  140.8 8.3 %all-to-all-done.2 = f32[64,2,1,8]{3,1,2,0:T(2,128)S(1)} async-done(((f32[64,2,1,8]{3,1,2,0:T(2,128)}), f32[64,2,1,8]{3,1,2,0:T(2,128)S(1)}, u32[]{:S(2)}, u32[]{:S(2)}) %all-to-all-start.2) | async-done | bytes 4128 | tf_op jit(solution)/shard_map/all_to_all | solution.py:167
  149.1 4.6 %all-to-all-start = ((f32[64,2,1,8,128]{4,3,1,2,0:T(8,128)}), f32[64,2,1,8,128]{4,3,1,2,0:T(8,128)S(1)}, u32[]{:S(2)}, u32[]{:S(2)}) async-start(f32[64,2,1,8,128]{4,3,1,2,0:T(8,128)} %bitcast.44), calls=%async_computation | async-start | bytes 1048576 | tf_op jit(solution)/shard_map/all_to_all | solution.py:165
  154.4 16.5 %all-to-all-done = f32[64,2,1,8,128]{4,3,1,2,0:T(8,128)S(1)} async-done(((f32[64,2,1,8,128]{4,3,1,2,0:T(8,128)}), f32[64,2,1,8,128]{4,3,1,2,0:T(8,128)S(1)}, u32[]{:S(2)}, u32[]{:S(2)}) %all-to-all-start) | async-done | bytes 524320 | tf_op jit(solution)/shard_map/all_to_all | solution.py:165
  171.3 78.1 %all-gather.1 = bf16[64,2,1024]{2,1,0:T(2,128)(2,1)S(1)} all-gather(bf16[1,2,1024]{2,1,0:T(2,128)(2,1)S(1)} %reshape.312), channel_id=1, replica_groups=mesh['agents'=64,'heads'=8] {'agents'}, dimensions={0}, use_global_device_ids=true | all-gather | bytes 266240 | tf_op jit(solution)/shard_map/all_gather | solution.py:178
  249.5 0.8 convolution_convert_fusion
  250.4 71.4 %reduce-scatter.2.cloned.1.call-done = bf16[16,128]{1,0:T(8,128)(2,1)} async-done(((bf16[128,128]{1,0:T(8,128)(2,1)}), bf16[16,128]{1,0:T(8,128)(2,1)}) %reduce-scatter.2.cloned.1.call-update) | async-done | bytes 4112 | tf_op jit(solution)/shard_map/reduce_scatter | solution.py:182
  (66 shorter events, 8.6 us)
Async XLA Ops:
  6.5 243.0 %copy-start = (bf16[1024,128]{1,0:T(8,128)(2,1)S(1)}, bf16[1024,128]{1,0:T(8,128)(2,1)}, u32[]{:S(2)}) copy-start(bf16[1024,128]{1,0:T(8,128)(2,1)} %param.21) | copy-start | bytes 786436
  6.5 98.1 %copy-start.1 = (bf16[2,2048,128]{2,1,0:T(8,128)(2,1)S(1)}, bf16[2,2048,128]{2,1,0:T(8,128)(2,1)}, u32[]{:S(2)}) copy-start(bf16[2,2048,128]{2,1,0:T(8,128)(2,1)} %param.15) | copy-start | bytes 3145732
  100.1 0.7 copy-start.5
  107.5 1.0 copy-start.2
  116.7 17.1 %all-to-all-start.1 = ((f32[64,2,1,8]{3,1,2,0:T(2,128)}), f32[64,2,1,8]{3,1,2,0:T(2,128)S(1)}, u32[]{:S(2)}, u32[]{:S(2)}) async-start(f32[64,2,1,8]{3,1,2,0:T(2,128)} %bitcast.47), calls=%async_computation.1 | async-start | bytes 131072 | tf_op jit(solution)/shard_map/all_to_all | solution.py:166
  133.8 15.2 %all-to-all-start.2 = ((f32[64,2,1,8]{3,1,2,0:T(2,128)}), f32[64,2,1,8]{3,1,2,0:T(2,128)S(1)}, u32[]{:S(2)}, u32[]{:S(2)}) async-start(f32[64,2,1,8]{3,1,2,0:T(2,128)} %bitcast.55), calls=%async_computation.2 | async-start | bytes 131072 | tf_op jit(solution)/shard_map/all_to_all | solution.py:167
  149.1 4.7 %copy-start.6 = (s32[2]{0:T(128)S(1)}, s32[2]{0:T(128)}, u32[]{:S(2)}) copy-start(s32[2]{0:T(128)} %param.19) | copy-start | bytes 28
  149.1 4.7 %copy-start.3 = (bf16[2,2,128,128]{3,2,1,0:T(8,128)(2,1)S(1)}, bf16[2,2,128,128]{3,2,1,0:T(8,128)(2,1)}, u32[]{:S(2)}) copy-start(bf16[2,2,128,128]{3,2,1,0:T(8,128)(2,1)} %param.16) | copy-start | bytes 393220
  149.1 4.7 %copy-start.4 = (bf16[2,1024]{1,0:T(2,128)(2,1)S(1)}, bf16[2,1024]{1,0:T(2,128)(2,1)}, u32[]{:S(2)}) copy-start(bf16[2,1024]{1,0:T(2,128)(2,1)} %param.13) | copy-start | bytes 12292
  149.1 21.9 %all-to-all-start = ((f32[64,2,1,8,128]{4,3,1,2,0:T(8,128)}), f32[64,2,1,8,128]{4,3,1,2,0:T(8,128)S(1)}, u32[]{:S(2)}, u32[]{:S(2)}) async-start(f32[64,2,1,8,128]{4,3,1,2,0:T(8,128)} %bitcast.44), calls=%async_computation | async-start | bytes 1048576 | tf_op jit(solution)/shard_map/all_to_all | solution.py:165
  153.7 168.1 %reduce-scatter.2.cloned.1.call-start = ((), (), s32[]{:S(2)}) async-start(), calls=%async_computation.4 | async-start | bytes 36864 | tf_op jit(solution)/shard_map/reduce_scatter | solution.py:182
Sparse Core Ops, SparseCore 0:
  250.5 71.2 reduce-scatter.1
where the time goes:
time: 330 us; the launch traced here: 329 us
  blocking collectives  166 us (50%)
  waiting for transfers between devices  102 us (31%)
  starting transfers between devices  17 us (5%)
  between operations  16.1 us (5%)
  other arithmetic  12.7 us (4%)
  local copies, waits for them, and re-layouts  9.8 us (3%)
  matrix products  5.07 us (2%)
    all_gather x1, blocking collectives, shards(): gathered = lax.all_gather(queries, 'agents', axis=0, tiled=True)  88 us
    all_gather x1, blocking collectives, shards(): lax.all_gather(attention, 'agents', axis=0, tiled=True)  78.1 us
    reduce_scatter x1, waiting for transfers between devices, shards(): lax.psum_scatter(projected.astype(jnp.bfloat16), 'heads', scatter_dimensi...  71.4 us
    all_to_all x1, waiting for transfers between devices, shards(): lax.all_to_all(outgoing[0], 'agents', split_axis=0, concat_axis=0, tiled=...  16.5 us
    all_to_all x1, waiting for transfers between devices, shards(): lax.all_to_all(outgoing[2], 'agents', split_axis=0, concat_axis=0, tiled=...  8.3 us
    all_to_all x1, starting transfers between devices, shards(): lax.all_to_all(outgoing[1], 'agents', split_axis=0, concat_axis=0, tiled=...  7.1 us
  transfers between devices with their start and end apart: 4, of which 4 were waited for; matrix products, arithmetic and copies ran while one was open for 2% of the time, Pallas kernels for 0%

commit v1 on v0

v1 whole, which is shorter than its diff:
```python
import math

import jax
import jax.numpy as jnp
from jax import lax
from jax.experimental import pallas as pl
from jax.experimental.pallas import tpu as pltpu
from jax.sharding import PartitionSpec as P

HEAD_DIM = 128
TEAM_CAP = 8
NEG = -1e30
MESH = pl.DeviceIdType.MESH
F32 = jnp.float32
BF16 = jnp.bfloat16


def dot(a, b):
    return jnp.dot(a, b, preferred_element_type=F32)


def dot_t(a, b):
    return lax.dot_general(a, b, (((1,), (1,)), ((), ())), preferred_element_type=F32)


def iota(shape, dim):
    return lax.broadcasted_iota(jnp.int32, shape, dim)


def softmax_part(scores, values, scaling):
    high = jnp.max(scores, axis=-1, keepdims=True)
    weights = jnp.exp((scores - high) * scaling)
    mass = jnp.sum(weights, axis=-1, keepdims=True)
    return dot(weights.astype(BF16), values), high, mass


def make_kernel(agent_devices, head_devices):
    chips = agent_devices // 2
    rows = chips * 16

    def kernel(
        q_ref, lengths_ref, map_ref, owner_ref, suffix_len_ref,
        global_hbm, team_hbm, suffix_hbm, weight_hbm,
        out_ref,
        q_f32, q_own, q_all, global_kv, team_kv, suffix_kv, weight,
        part_out, part_in, lse_out, lse_in, att_own, att_all, att_f32,
        proj_out, proj_in, merged,
        local_sem, send_sem, recv_sem,
    ):
        a = lax.axis_index("agents")
        h = lax.axis_index("heads")
        core = lax.rem(a, 2)
        chip = a // 2
        scaling = 1.0 / math.sqrt(HEAD_DIM)

        def same_core(k):
            return (lax.rem(chip + k, chips) * 2 + core, h)

        def head_peer(k, d):
            return (chip * 2 + lax.rem(core + d, 2), lax.rem(h + k, head_devices))

        sibling = head_peer(0, 1)
        peers = [same_core(k) for k in range(1, chips)]
        heads = [(k, d) for k in range(head_devices) for d in range(2) if k or d]

        barrier = pltpu.get_barrier_semaphore()
        for peer in peers + [head_peer(k, d) for k, d in heads]:
            pl.semaphore_signal(barrier, inc=1, device_id=peer, device_id_type=MESH)

        span = global_hbm.shape[1]
        own_span = pl.ds(pl.multiple_of(core * span, span), span)
        local = [
            pltpu.make_async_copy(global_hbm, global_kv.at[:, own_span], local_sem.at[0]),
            pltpu.make_async_copy(team_hbm, team_kv.at[core], local_sem.at[1]),
            pltpu.make_async_copy(suffix_hbm, suffix_kv, local_sem.at[2]),
            pltpu.make_async_copy(weight_hbm, weight.at[core], local_sem.at[3]),
        ]
        for copy in local:
            copy.start()

        for i in range(2):
            for j in range(8):
                q_f32[pl.ds(i * 8 + j, 1), :] = q_ref[
                    pl.ds(i, 1), pl.ds(j * HEAD_DIM, HEAD_DIM)
                ].astype(F32)
        q_own[...] = q_f32[...].astype(BF16)

        pl.semaphore_wait(barrier, len(peers) + len(heads))

        own_rows = pl.ds(pl.multiple_of(chip * 16, 16), 16)

        def send(src, dst, s, peer):
            copy = pltpu.make_async_remote_copy(
                src_ref=src, dst_ref=dst, send_sem=send_sem.at[s], recv_sem=recv_sem.at[s],
                device_id=peer, device_id_type=MESH,
            )
            copy.start()

        def keep(src, dst, s):
            pltpu.make_async_copy(src, dst, recv_sem.at[s]).start()

        def arrived(ref, s):
            pltpu.make_async_copy(ref, ref, recv_sem.at[s]).wait()

        def sent(ref, s):
            pltpu.make_async_copy(ref, ref, send_sem.at[s]).wait()

        for peer in peers:
            send(q_own, q_all.at[own_rows], 0, peer)
        keep(q_own, q_all.at[own_rows], 0)
        send(global_hbm, global_kv.at[:, own_span], 1, sibling)
        send(team_hbm, team_kv.at[core], 2, sibling)
        send(weight_hbm, weight.at[core], 3, sibling)

        agents = map_ref.shape[1]
        team_of = map_ref[...]
        agent = iota((1, agents), 1)
        mine = lax.rem(agent // 2, 2) == core
        before = (iota((agents, agents), 0) < iota((agents, agents), 1)).astype(BF16)
        row_agent = iota((agents, rows), 1)
        row_agent = (row_agent // 16) * 4 + core * 2 + (row_agent // 8) % 2
        spread = (iota((agents, rows), 0) == row_agent).astype(BF16)
        owner = owner_ref[...]
        team_ids = iota(owner.shape, 1)
        picks, spans = [], []
        for slot in range(2):
            here = owner == chip * 2 + slot
            team = jnp.sum(jnp.where(here, team_ids, 0), axis=1, keepdims=True)
            spans.append(jnp.sum(jnp.where(here, lengths_ref[...], 0), axis=1, keepdims=True))
            member = jnp.logical_and(team_of == team, mine)
            members = jnp.broadcast_to(jnp.where(member, 1.0, 0.0), (8, agents)).astype(BF16)
            rank = dot(members, before)[0:1]
            code = jnp.where(member, rank, 255.0)
            picks.append(dot(jnp.broadcast_to(code, (8, agents)).astype(BF16), spread)[0:1])
        place = iota((TEAM_CAP * 8, rows), 0)
        same_head = place % 8 == iota((TEAM_CAP * 8, rows), 1) % 8
        take = jnp.concatenate(
            [
                jnp.where(
                    jnp.logical_and(code == (place // 8).astype(F32), same_head), 1.0, 0.0
                )
                for code in picks
            ],
            axis=0,
        )
        give = take.T
        take = take.astype(BF16)

        local[2].wait()
        suffix_num, suffix_lse = [], []
        for i in range(2):
            scores = dot_t(q_own[...], suffix_kv[0, i])[i * 8 : i * 8 + 8]
            seen = iota(scores.shape, 1) < suffix_len_ref[i]
            high = jnp.max(jnp.where(seen, scores, NEG), axis=-1, keepdims=True)
            weights = jnp.where(seen, jnp.exp((jnp.minimum(scores, high) - high) * scaling), 0.0)
            mass = jnp.sum(weights, axis=-1, keepdims=True)
            weights = jnp.concatenate([weights, weights], axis=0).astype(BF16)
            num = dot(weights, suffix_kv[1, i])[0:8]
            suffix_num.append(num / mass)
            suffix_lse.append(high * scaling + jnp.log(mass))
        suffix_num = jnp.concatenate(suffix_num, axis=0)
        suffix_lse = jnp.concatenate(suffix_lse, axis=0)

        local[0].wait()
        local[1].wait()
        arrived(global_hbm, 1)
        arrived(team_hbm, 2)
        arrived(q_all, 0)

        team_rows = dot(take, q_all[...]).astype(BF16)
        team_num, team_high, team_mass = [], [], []
        for slot in range(2):
            block = TEAM_CAP * 8
            scores = dot_t(team_rows[slot * block : slot * block + block], team_kv[slot, 0])
            scores = jnp.where(iota(scores.shape, 1) < spans[slot], scores, NEG)
            num, high, mass = softmax_part(scores, team_kv[slot, 1], scaling)
            team_num.append(num)
            team_high.append(high)
            team_mass.append(mass)
        team_num = jnp.concatenate(team_num, axis=0)
        team_high = jnp.concatenate(team_high, axis=0)
        team_mass = jnp.concatenate(team_mass, axis=0)
        eye = iota((128, 128), 0) == iota((128, 128), 1)
        high_lane = jnp.max(jnp.where(eye, team_high, NEG), axis=0, keepdims=True)
        mass_lane = jnp.sum(jnp.where(eye, team_mass, 0.0), axis=0, keepdims=True)
        coarse = team_num.astype(BF16)
        fine = (team_num - coarse.astype(F32)).astype(BF16)

        chunk = 128
        for c in range(rows // chunk):
            span_rows = pl.ds(c * chunk, chunk)
            scores = dot_t(q_all[span_rows, :], global_kv[0])
            num, high, mass = softmax_part(scores, global_kv[1], scaling)
            chosen = give[c * chunk : c * chunk + chunk]
            is_team = chosen > 0.5
            t_high = jnp.max(jnp.where(is_team, high_lane, NEG), axis=-1, keepdims=True)
            t_mass = jnp.sum(jnp.where(is_team, mass_lane, 0.0), axis=-1, keepdims=True)
            chosen = chosen.astype(BF16)
            t_num = dot(chosen, coarse) + dot(chosen, fine)
            top = jnp.maximum(high, t_high)
            g_factor = jnp.exp((high - top) * scaling)
            t_factor = jnp.exp((t_high - top) * scaling)
            mass = mass * g_factor + t_mass * t_factor
            num = (num * g_factor + t_num * t_factor) / mass
            part_out[span_rows, :] = num.astype(BF16)
            lse = jnp.where(
                iota((chunk, 128), 1) == iota((chunk, 128), 0) % 16, top * scaling + jnp.log(mass), 0.0
            )
            lse_out[pl.ds(c * chunk // 16, chunk // 16)] = jnp.sum(
                lse.reshape(chunk // 16, 16, 128), axis=1, keepdims=True
            )

        for k in range(1, chips):
            to = lax.rem(chip + k, chips)
            send(part_out.at[pl.ds(pl.multiple_of(to * 16, 16), 16)], part_in.at[own_rows], 4, peers[k - 1])
            send(lse_out.at[to], lse_in.at[chip], 5, peers[k - 1])
        keep(part_out.at[own_rows], part_in.at[own_rows], 4)
        keep(lse_out.at[chip], lse_in.at[chip], 5)
        arrived(lse_in, 5)
        lse = lse_in[...].reshape(chips, 128)
        lse = jnp.concatenate([lse, jnp.full((128 - chips, 128), NEG, F32)], axis=0).T[0:16]
        top = jnp.maximum(jnp.max(lse, axis=-1, keepdims=True), suffix_lse)
        factors = jnp.exp(lse - top)
        suffix_factor = jnp.exp(suffix_lse - top)
        total = jnp.sum(factors, axis=-1, keepdims=True) + suffix_factor
        num = suffix_num * suffix_factor
        arrived(part_in, 4)
        for j in range(chips):
            num = num + part_in[pl.ds(j * 16, 16), :].astype(F32) * factors[:, j : j + 1]
        att_own[...] = (num / total).astype(BF16)

        for peer in peers:
            send(att_own, att_all.at[own_rows], 6, peer)
        keep(att_own, att_all.at[own_rows], 6)
        local[3].wait()
        arrived(weight_hbm, 3)
        arrived(att_all, 6)
        att_f32[...] = att_all[...].astype(F32)
        att = jnp.concatenate(
            [att_f32[pl.ds(j, rows // 8, stride=8), :] for j in range(8)], axis=1
        ).astype(BF16)
        for side in range(2):
            proj_out[:, side] = dot(att, weight[side]).reshape(head_devices, rows // 8 // head_devices, 128)

        for k, d in heads:
            to = (lax.rem(h + k, head_devices), lax.rem(core + d, 2))
            send(proj_out.at[to[0], to[1]], proj_in.at[h, core], 7, head_peer(k, d))
        keep(proj_out.at[h, core], proj_in.at[h, core], 7)
        arrived(proj_in, 7)
        summed = jnp.sum(proj_in[...], axis=0)
        for side in range(2):
            for j in range(4):
                merged[pl.ds(4 * j + 2 * side, 2), :] = summed[side, 2 * j : 2 * j + 2]
        out_ref[...] = merged[...].astype(BF16)

        others = pl.ds(0, (chips - 1) * 16)
        sent(q_all.at[others], 0)
        sent(global_hbm, 1)
        sent(team_hbm, 2)
        sent(weight_hbm, 3)
        sent(part_in.at[others], 4)
        sent(lse_in.at[pl.ds(0, chips - 1)], 5)
        sent(att_all.at[others], 6)
        sent(att_f32.at[pl.ds(0, len(heads) * 8)], 7)

    return kernel, rows, chips


def shards(queries, global_kv, team_kv, suffix_kv, team_lengths, team_map, suffix_lengths, team_owner, out_weight):
    agent_devices = lax.axis_size("agents")
    head_devices = lax.axis_size("heads")
    kernel, rows, chips = make_kernel(agent_devices, head_devices)
    vmem = pl.BlockSpec(memory_space=pltpu.VMEM)
    hbm = pl.BlockSpec(memory_space=pl.ANY)
    span = global_kv.shape[1]
    out_rows = rows * 2 // 8 // head_devices
    return pl.pallas_call(
        kernel,
        out_shape=jax.ShapeDtypeStruct((out_rows, out_weight.shape[1]), BF16),
        in_specs=[vmem] * 4 + [pl.BlockSpec(memory_space=pltpu.SMEM)] + [hbm] * 4,
        out_specs=vmem,
        scratch_shapes=[
            pltpu.VMEM((16, 128), F32),
            pltpu.VMEM((16, 128), BF16),
            pltpu.VMEM((rows, 128), BF16),
            pltpu.VMEM((2, 2 * span, 128), BF16),
            pltpu.VMEM((2,) + team_kv.shape, BF16),
            pltpu.VMEM(suffix_kv.shape, BF16),
            pltpu.VMEM((2,) + out_weight.shape, BF16),
            pltpu.VMEM((rows, 128), BF16),
            pltpu.VMEM((rows, 128), BF16),
            pltpu.VMEM((chips, 1, 128), F32),
            pltpu.VMEM((chips, 1, 128), F32),
            pltpu.VMEM((16, 128), BF16),
            pltpu.VMEM((rows, 128), BF16),
            pltpu.VMEM((rows, 128), F32),
            pltpu.VMEM((head_devices, 2, 8, 128), F32),
            pltpu.VMEM((head_devices, 2, 8, 128), F32),
            pltpu.VMEM((16, 128), F32),
            pltpu.SemaphoreType.DMA((4,)),
            pltpu.SemaphoreType.DMA((8,)),
            pltpu.SemaphoreType.DMA((8,)),
        ],
        compiler_params=pltpu.CompilerParams(
            collective_id=0, has_side_effects=True, vmem_limit_bytes=48 * 1024 * 1024
        ),
        name="decode",
    )(
        queries,
        team_lengths.reshape(1, -1),
        team_map.reshape(1, -1),
        team_owner.reshape(1, -1),
        suffix_lengths,
        global_kv,
        team_kv,
        suffix_kv,
        out_weight,
    )


def solution(mesh):
    return jax.shard_map(
        shards,
        mesh=mesh,
        in_specs=(
            P("agents", "heads"),
            P(None, "agents", "heads"),
            P(None, "agents", "heads"),
            P(None, "agents", None, "heads"),
            P(),
            P(),
            P("agents"),
            P(),
            P("heads", "agents"),
        ),
        out_specs=P("heads", "agents"),
        check_vma=False,
    )
```

time: 330 us -> 52.6 us (0.16)
  blocking collectives: 166 us -> 0 us
  waiting for transfers between devices: 102 us -> 0 us
  Pallas kernels: 0 us -> 46.3 us
  starting transfers between devices: 17 us -> 0 us
  between operations: 16.1 us -> 0.03 us
  other arithmetic: 12.7 us -> 0 us
  matrix products: 5.07 us -> 0 us
  local copies, waits for them, and re-layouts: 9.8 us -> 5.97 us
    all_gather x2 -> x0, blocking collectives: 166 us -> none  [the longest x1 88 us: shards(): gathered = lax.all_gather(queries, 'agents', axis=0, tiled=True)]
    reduce_scatter x1 -> x0, waiting for transfers between devices: 71.4 us -> none  [shards(): lax.psum_scatter(projected.astype(jnp.bfloat16), 'heads', scatter_dimensi...]
    pallas_call x0 -> x1, Pallas kernels: none -> 46.3 us  [shards(): pl.pallas_call(kernel, out_shape=jax.ShapeDtypeStruct((out_rows, out_weig...]
    all_to_all x3 -> x0, waiting for transfers between devices: 30.3 us -> none  [the longest x1 16.5 us: shards(): lax.all_to_all(outgoing[0], 'agents', split_axis=0, concat_axis=0, tiled=...]
    all_to_all x3 -> x0, starting transfers between devices: 17 us -> none  [the longest x1 7.1 us: shards(): lax.all_to_all(outgoing[1], 'agents', split_axis=0, concat_axis=0, tiled=...]
    dot_general x11 -> x0, matrix products: 5.07 us -> none  [the longest x4 2.56 us: key_partial(): jnp.einsum('ajgt,tjd->ajgd', weights.astype(jnp.bfloat16), value_block, p...]
    scatter x2 -> x0, other arithmetic: 5.02 us -> none  [the longest x1 2.98 us: fold_rows(): weight_sum.at[target].set(merged[2], mode='drop')]
    unnamed x16 -> x19, local copies, waits for them, and re-layouts: 1.05 us -> 5.97 us
  transfers between devices with their start and end apart: 4 -> 0, of which waited for: 4 -> 0; matrix products, arithmetic and copies ran while one was open for 2% -> 0% of each run, Pallas kernels for 0% -> 0%
where the time goes in v1:
time: 52.6 us; the launch traced here: 52.3 us
  Pallas kernels  46.3 us (88%)
  local copies, waits for them, and re-layouts  5.97 us (11%)
    pallas_call x1, Pallas kernels, shards(): pl.pallas_call(kernel, out_shape=jax.ShapeDtypeStruct((out_rows, out_weig...  46.3 us
    unnamed x19, local copies, waits for them, and re-layouts  5.97 us

profile of v1, /device:TPU:1, one launch (start us, length us, event | category | flops | bytes accessed | tf_op | source)
XLA Modules:
  0.0 52.3 jit_solution(7145940273172497359)
XLA Ops:
  0.0 0.0 copy-start.4
  0.0 0.0 copy-start.5
  0.0 0.0 copy-start.6
  0.0 0.0 copy-start.7
  0.0 0.7 %copy-done.4 = bf16[2,1024]{1,0:T(2,128)(2,1)S(1)} copy-done((bf16[2,1024]{1,0:T(2,128)(2,1)S(1)}, bf16[2,1024]{1,0:T(2,128)(2,1)}, u32[]{:S(2)}) %copy-start.4) | copy-done | bytes 4120
  0.7 0.0 copy-done.5
  0.7 0.0 copy-done.6
  0.7 0.0 copy-done.7
  0.7 0.0 copy-start
  0.7 1.2 %copy-done = bf16[2,2048,128]{2,1,0:T(8,128)(2,1)S(1)} copy-done((bf16[2,2048,128]{2,1,0:T(8,128)(2,1)S(1)}, bf16[2,2048,128]{2,1,0:T(8,128)(2,1)}, u32[]{:S(2)}) %copy-start) | copy-done | bytes 1048600
  1.9 0.0 copy-start.1
  1.9 0.9 %copy-done.1 = bf16[2,512,128]{2,1,0:T(8,128)(2,1)S(1)} copy-done((bf16[2,512,128]{2,1,0:T(8,128)(2,1)S(1)}, bf16[2,512,128]{2,1,0:T(8,128)(2,1)}, u32[]{:S(2)}) %copy-start.1) | copy-done | bytes 262168
  2.9 0.0 copy-start.2
  2.9 0.9 %copy-done.2 = bf16[1024,128]{1,0:T(8,128)(2,1)S(1)} copy-done((bf16[1024,128]{1,0:T(8,128)(2,1)S(1)}, bf16[1024,128]{1,0:T(8,128)(2,1)}, u32[]{:S(2)}) %copy-start.2) | copy-done | bytes 262168
  3.8 0.0 copy-start.3
  3.8 0.9 %copy-done.3 = bf16[2,2,128,128]{3,2,1,0:T(8,128)(2,1)S(1)} copy-done((bf16[2,2,128,128]{3,2,1,0:T(8,128)(2,1)S(1)}, bf16[2,2,128,128]{3,2,1,0:T(8,128)(2,1)}, u32[]{:S(2)}) %copy-start.3) | copy-done | bytes 131096
  4.7 0.0 copy-start.8
  4.7 0.7 %copy-done.8 = s32[2]{0:T(128)S(1)} copy-done((s32[2]{0:T(128)S(1)}, s32[2]{0:T(128)}, u32[]{:S(2)}) %copy-start.8) | copy-done | bytes 32
  5.4 46.3 %decode.1 = bf16[16,128]{1,0:T(8,128)(2,1)S(1)} custom-call(bf16[2,1024]{1,0:T(2,128)(2,1)S(1)} %copy-done.4, s32[1,64]{1,0:T(1,128)S(1)} %bitcast.3, s32[1,128]{1,0:T(1,128)S(1)} %bitcast.4, s32[1,64]{1,0:T(1,128)S(1)} %bitcast.5, s32[2]{0:T(128)S(1)} %copy-done.8, bf16[2,512,128]{2,1,0:T(8,128)(2,1)S(1)} %copy-done.1, bf16[2,2048,128]{2,1,0:T(8,128)(2,1)S(1)} %copy-done, ...), custom_call_target="tpu_custom_call" | custom-call | tf_op jit(solution)/shard_map/decode/pallas_call | solution.py:277
  51.7 0.6 %copy.11 = bf16[16,128]{1,0:T(8,128)(2,1)} copy(bf16[16,128]{1,0:T(8,128)(2,1)S(1)} %decode.1) | data formatting | bytes 8192
Async XLA Ops:
  0.0 0.7 %copy-start.4 = (bf16[2,1024]{1,0:T(2,128)(2,1)S(1)}, bf16[2,1024]{1,0:T(2,128)(2,1)}, u32[]{:S(2)}) copy-start(bf16[2,1024]{1,0:T(2,128)(2,1)} %q_ref.1) | copy-start | bytes 12292
  0.0 0.7 %copy-start.5 = (s32[64]{0:T(128)S(1)}, s32[64]{0:T(128)}, u32[]{:S(2)}) copy-start(s32[64]{0:T(128)} %param.13) | copy-start | bytes 772
  0.0 0.7 %copy-start.6 = (s32[128]{0:T(128)S(1)}, s32[128]{0:T(128)}, u32[]{:S(2)}) copy-start(s32[128]{0:T(128)} %param.14) | copy-start | bytes 1540
  0.0 0.7 %copy-start.7 = (s32[64]{0:T(128)S(1)}, s32[64]{0:T(128)}, u32[]{:S(2)}) copy-start(s32[64]{0:T(128)} %param.16) | copy-start | bytes 772
  0.7 1.2 %copy-start = (bf16[2,2048,128]{2,1,0:T(8,128)(2,1)S(1)}, bf16[2,2048,128]{2,1,0:T(8,128)(2,1)}, u32[]{:S(2)}) copy-start(bf16[2,2048,128]{2,1,0:T(8,128)(2,1)} %team_hbm.1) | copy-start | bytes 3145732
  1.9 0.9 %copy-start.1 = (bf16[2,512,128]{2,1,0:T(8,128)(2,1)S(1)}, bf16[2,512,128]{2,1,0:T(8,128)(2,1)}, u32[]{:S(2)}) copy-start(bf16[2,512,128]{2,1,0:T(8,128)(2,1)} %global_hbm.1) | copy-start | bytes 786436
  2.9 0.9 %copy-start.2 = (bf16[1024,128]{1,0:T(8,128)(2,1)S(1)}, bf16[1024,128]{1,0:T(8,128)(2,1)}, u32[]{:S(2)}) copy-start(bf16[1024,128]{1,0:T(8,128)(2,1)} %weight_hbm.1) | copy-start | bytes 786436
  3.8 0.9 %copy-start.3 = (bf16[2,2,128,128]{3,2,1,0:T(8,128)(2,1)S(1)}, bf16[2,2,128,128]{3,2,1,0:T(8,128)(2,1)}, u32[]{:S(2)}) copy-start(bf16[2,2,128,128]{3,2,1,0:T(8,128)(2,1)} %suffix_hbm.1) | copy-start | bytes 393220
  4.7 0.7 %copy-start.8 = (s32[2]{0:T(128)S(1)}, s32[2]{0:T(128)}, u32[]{:S(2)}) copy-start(s32[2]{0:T(128)} %suffix_len_ref.1) | copy-start | bytes 28

commit v2 on v1

--- a/solution.py
+++ b/solution.py
@@ -9,6 +9,7 @@
 
 HEAD_DIM = 128
 TEAM_CAP = 8
+RING = 8
 NEG = -1e30
 MESH = pl.DeviceIdType.MESH
 F32 = jnp.float32
@@ -39,45 +40,66 @@
     rows = chips * 16
 
     def kernel(
-        q_ref, lengths_ref, map_ref, owner_ref, suffix_len_ref,
+        q_hbm, lengths_hbm, map_hbm, owner_hbm, suffix_len_hbm,
         global_hbm, team_hbm, suffix_hbm, weight_hbm,
         out_ref,
-        q_f32, q_own, q_all, global_kv, team_kv, suffix_kv, weight,
+        q_ref, lengths_ref, map_ref, owner_ref, suffix_len_ref, q_f32, q_own, q_all, global_kv, team_kv, suffix_kv, weight,
         part_out, part_in, lse_out, lse_in, att_own, att_all, att_f32,
         proj_out, proj_in, merged,
-        local_sem, send_sem, recv_sem,
+        local_sem, send_sem, recv_sem, word,
     ):
         a = lax.axis_index("agents")
         h = lax.axis_index("heads")
         core = lax.rem(a, 2)
         chip = a // 2
+        ring = RING
+        lines = chips // ring
+        z = lax.rem(chip, ring)
+        y = chip // ring
+        plane = lines * 16
         scaling = 1.0 / math.sqrt(HEAD_DIM)
-
-        def same_core(k):
-            return (lax.rem(chip + k, chips) * 2 + core, h)
+        steps = [(s + 1) // 2 if s % 2 else (ring - s // 2) % ring for s in range(ring)]
+
+        def at(dy, dz):
+            return ((lax.rem(y + dy, lines) * ring + lax.rem(z + dz, ring)) * 2 + core, h)
 
         def head_peer(k, d):
             return (chip * 2 + lax.rem(core + d, 2), lax.rem(h + k, head_devices))
 
         sibling = head_peer(0, 1)
-        peers = [same_core(k) for k in range(1, chips)]
+        line_peers = [at(k, 0) for k in range(1, lines)]
+        ring_peers = [at(0, k) for k in range(1, ring)]
         heads = [(k, d) for k in range(head_devices) for d in range(2) if k or d]
 
         barrier = pltpu.get_barrier_semaphore()
-        for peer in peers + [head_peer(k, d) for k, d in heads]:
+        greeted = line_peers + ring_peers + [sibling]
+        for peer in greeted:
             pl.semaphore_signal(barrier, inc=1, device_id=peer, device_id_type=MESH)
+
+        @pl.when(z == 0)
+        def _():
+            for k in range(1, head_devices):
+                pl.semaphore_signal(barrier, inc=1, device_id=head_peer(k, 0), device_id_type=MESH)
 
         span = global_hbm.shape[1]
         own_span = pl.ds(pl.multiple_of(core * span, span), span)
+        small = [
+            pltpu.make_async_copy(q_hbm, q_ref, local_sem.at[4]),
+            pltpu.make_async_copy(lengths_hbm, lengths_ref, local_sem.at[5]),
+            pltpu.make_async_copy(map_hbm, map_ref, local_sem.at[6]),
+            pltpu.make_async_copy(owner_hbm, owner_ref, local_sem.at[7]),
+            pltpu.make_async_copy(suffix_len_hbm, suffix_len_ref, local_sem.at[8]),
+        ]
         local = [
             pltpu.make_async_copy(global_hbm, global_kv.at[:, own_span], local_sem.at[0]),
             pltpu.make_async_copy(team_hbm, team_kv.at[core], local_sem.at[1]),
             pltpu.make_async_copy(suffix_hbm, suffix_kv, local_sem.at[2]),
             pltpu.make_async_copy(weight_hbm, weight.at[core], local_sem.at[3]),
         ]
-        for copy in local:
+        for copy in small + local:
             copy.start()
 
+        small[0].wait()
         for i in range(2):
             for j in range(8):
                 q_f32[pl.ds(i * 8 + j, 1), :] = q_ref[
@@ -85,9 +107,16 @@
                 ].astype(F32)
         q_own[...] = q_f32[...].astype(BF16)
 
-        pl.semaphore_wait(barrier, len(peers) + len(heads))
+        @pl.when(z == 0)
+        def _():
+            pl.semaphore_wait(barrier, len(greeted) + head_devices - 1)
+
+        @pl.when(z != 0)
+        def _():
+            pl.semaphore_wait(barrier, len(greeted))
 
         own_rows = pl.ds(pl.multiple_of(chip * 16, 16), 16)
+        own_line = pl.ds(pl.multiple_of(y * 16, 16), 16)
 
         def send(src, dst, s, peer):
             copy = pltpu.make_async_remote_copy(
@@ -105,12 +134,21 @@
         def sent(ref, s):
             pltpu.make_async_copy(ref, ref, send_sem.at[s]).wait()
 
-        for peer in peers:
-            send(q_own, q_all.at[own_rows], 0, peer)
-        keep(q_own, q_all.at[own_rows], 0)
+        for peer in line_peers:
+            send(q_own, q_all.at[own_line], 0, peer)
+        keep(q_own, q_all.at[own_line], 0)
         send(global_hbm, global_kv.at[:, own_span], 1, sibling)
         send(team_hbm, team_kv.at[core], 2, sibling)
         send(weight_hbm, weight.at[core], 3, sibling)
+
+        own_plane = q_all.at[pl.ds(0, plane)]
+        arrived(own_plane, 0)
+        for slot in reversed(range(1, ring)):
+            there = steps.index((ring - steps[slot]) % ring)
+            send(own_plane, q_all.at[pl.ds(there * plane, plane)], 8 + there // 2, at(0, steps[slot]))
+
+        for copy in small[1:]:
+            copy.wait()
 
         agents = map_ref.shape[1]
         team_of = map_ref[...]
@@ -118,7 +156,10 @@
         mine = lax.rem(agent // 2, 2) == core
         before = (iota((agents, agents), 0) < iota((agents, agents), 1)).astype(BF16)
         row_agent = iota((agents, rows), 1)
-        row_agent = (row_agent // 16) * 4 + core * 2 + (row_agent // 8) % 2
+        slot = row_agent // plane
+        step = jnp.where(slot % 2 == 1, (slot + 1) // 2, ring - slot // 2)
+        row_chip = (row_agent // 16) % lines * ring + (z + step) % ring
+        row_agent = row_chip * 4 + core * 2 + (row_agent // 8) % 2
         spread = (iota((agents, rows), 0) == row_agent).astype(BF16)
         owner = owner_ref[...]
         team_ids = iota(owner.shape, 1)
@@ -161,12 +202,19 @@
         suffix_num = jnp.concatenate(suffix_num, axis=0)
         suffix_lse = jnp.concatenate(suffix_lse, axis=0)
 
+        chunk = 2 * plane
+        chunks = rows // chunk
         local[0].wait()
+        arrived(global_hbm, 1)
+        prompt = []
+        for c in range(chunks):
+            first = c * chunk + (plane if c == 0 else 0)
+            arrived(q_all.at[pl.ds(first, (c + 1) * chunk - first)], 8 + c)
+            scores = dot_t(q_all[pl.ds(c * chunk, chunk), :], global_kv[0])
+            prompt.append(softmax_part(scores, global_kv[1], scaling))
+
         local[1].wait()
-        arrived(global_hbm, 1)
         arrived(team_hbm, 2)
-        arrived(q_all, 0)
-
         team_rows = dot(take, q_all[...]).astype(BF16)
         team_num, team_high, team_mass = [], [], []
         for slot in range(2):
@@ -186,11 +234,9 @@
         coarse = team_num.astype(BF16)
         fine = (team_num - coarse.astype(F32)).astype(BF16)
 
-        chunk = 128
-        for c in range(rows // chunk):
+        for c in range(chunks):
             span_rows = pl.ds(c * chunk, chunk)
-            scores = dot_t(q_all[span_rows, :], global_kv[0])
-            num, high, mass = softmax_part(scores, global_kv[1], scaling)
+            num, high, mass = prompt[c]
             chosen = give[c * chunk : c * chunk + chunk]
             is_team = chosen > 0.5
             t_high = jnp.max(jnp.where(is_team, high_lane, NEG), axis=-1, keepdims=True)
@@ -210,12 +256,16 @@
                 lse.reshape(chunk // 16, 16, 128), axis=1, keepdims=True
             )
 
-        for k in range(1, chips):
-            to = lax.rem(chip + k, chips)
-            send(part_out.at[pl.ds(pl.multiple_of(to * 16, 16), 16)], part_in.at[own_rows], 4, peers[k - 1])
-            send(lse_out.at[to], lse_in.at[chip], 5, peers[k - 1])
-        keep(part_out.at[own_rows], part_in.at[own_rows], 4)
-        keep(lse_out.at[chip], lse_in.at[chip], 5)
+        for slot in reversed(range(ring)):
+            for k in reversed(range(lines)):
+                if slot or k:
+                    block = slot * lines + lax.rem(y + k, lines)
+                    peer = at(k, steps[slot])
+                    send(part_out.at[pl.ds(pl.multiple_of(block * 16, 16), 16)], part_in.at[own_rows], 4, peer)
+                    send(lse_out.at[block], lse_in.at[chip], 5, peer)
+        keep(part_out.at[own_line], part_in.at[own_rows], 4)
+        keep(lse_out.at[y], lse_in.at[chip], 5)
+
         arrived(lse_in, 5)
         lse = lse_in[...].reshape(chips, 128)
         lse = jnp.concatenate([lse, jnp.full((128 - chips, 128), NEG, F32)], axis=0).T[0:16]
@@ -229,9 +279,20 @@
             num = num + part_in[pl.ds(j * 16, 16), :].astype(F32) * factors[:, j : j + 1]
         att_own[...] = (num / total).astype(BF16)
 
-        for peer in peers:
-            send(att_own, att_all.at[own_rows], 6, peer)
+        for slot in reversed(range(ring)):
+            for k in reversed(range(lines)):
+                if slot or k:
+                    send(att_own, att_all.at[own_rows], 6, at(k, steps[slot]))
         keep(att_own, att_all.at[own_rows], 6)
+
+        @pl.when(z == 0)
+        def _():
+            for k in range(1, head_devices):
+                pl.semaphore_signal(word.at[0], inc=1, device_id=head_peer(k, 0), device_id_type=MESH)
+            pl.semaphore_wait(word.at[0], head_devices - 1)
+            for peer in ring_peers:
+                pl.semaphore_signal(word.at[1], inc=1, device_id=peer, device_id_type=MESH)
+
         local[3].wait()
         arrived(weight_hbm, 3)
         arrived(att_all, 6)
@@ -240,28 +301,37 @@
             [att_f32[pl.ds(j, rows // 8, stride=8), :] for j in range(8)], axis=1
         ).astype(BF16)
         for side in range(2):
-            proj_out[:, side] = dot(att, weight[side]).reshape(head_devices, rows // 8 // head_devices, 128)
+            proj_out[pl.ds(side * head_devices, head_devices)] = (
+                dot(att, weight[side]).astype(BF16).reshape(head_devices, 8, 128)
+            )
+
+        @pl.when(z != 0)
+        def _():
+            pl.semaphore_wait(word.at[1], 1)
 
         for k, d in heads:
             to = (lax.rem(h + k, head_devices), lax.rem(core + d, 2))
-            send(proj_out.at[to[0], to[1]], proj_in.at[h, core], 7, head_peer(k, d))
-        keep(proj_out.at[h, core], proj_in.at[h, core], 7)
+            send(proj_out.at[to[1] * head_devices + to[0]], proj_in.at[core * head_devices + h], 7, head_peer(k, d))
+        keep(proj_out.at[core * head_devices + h], proj_in.at[core * head_devices + h], 7)
         arrived(proj_in, 7)
-        summed = jnp.sum(proj_in[...], axis=0)
         for side in range(2):
+            summed = jnp.sum(proj_in[pl.ds(side * head_devices, head_devices)].astype(F32), axis=0)
             for j in range(4):
-                merged[pl.ds(4 * j + 2 * side, 2), :] = summed[side, 2 * j : 2 * j + 2]
+                merged[pl.ds(4 * j + 2 * side, 2), :] = summed[2 * j : 2 * j + 2]
         out_ref[...] = merged[...].astype(BF16)
 
         others = pl.ds(0, (chips - 1) * 16)
-        sent(q_all.at[others], 0)
+        sent(q_all.at[pl.ds(0, plane - 16)], 0)
+        for c in range(chunks):
+            first = c * chunk + (plane if c == 0 else 0)
+            sent(q_all.at[pl.ds(first, (c + 1) * chunk - first)], 8 + c)
         sent(global_hbm, 1)
         sent(team_hbm, 2)
         sent(weight_hbm, 3)
         sent(part_in.at[others], 4)
         sent(lse_in.at[pl.ds(0, chips - 1)], 5)
         sent(att_all.at[others], 6)
-        sent(att_f32.at[pl.ds(0, len(heads) * 8)], 7)
+        sent(proj_in.at[pl.ds(0, len(heads))], 7)
 
     return kernel, rows, chips
 
@@ -271,15 +341,20 @@
     head_devices = lax.axis_size("heads")
     kernel, rows, chips = make_kernel(agent_devices, head_devices)
     vmem = pl.BlockSpec(memory_space=pltpu.VMEM)
-    hbm = pl.BlockSpec(memory_space=pl.ANY)
+    hbm = pl.BlockSpec(memory_space=pltpu.HBM)
     span = global_kv.shape[1]
     out_rows = rows * 2 // 8 // head_devices
     return pl.pallas_call(
         kernel,
-        out_shape=jax.ShapeDtypeStruct((out_rows, out_weight.shape[1]), BF16),
-        in_specs=[vmem] * 4 + [pl.BlockSpec(memory_space=pltpu.SMEM)] + [hbm] * 4,
+        out_shape=pltpu.VMEM((out_rows, out_weight.shape[1]), BF16),
+        in_specs=[hbm] * 9,
         out_specs=vmem,
         scratch_shapes=[
+            pltpu.VMEM(queries.shape, BF16),
+            pltpu.VMEM((1,) + team_lengths.shape, jnp.int32),
+            pltpu.VMEM((1,) + team_map.shape, jnp.int32),
+            pltpu.VMEM((1,) + team_owner.shape, jnp.int32),
+            pltpu.SMEM(suffix_lengths.shape, jnp.int32),
             pltpu.VMEM((16, 128), F32),
             pltpu.VMEM((16, 128), BF16),
             pltpu.VMEM((rows, 128), BF16),
@@ -294,15 +369,16 @@
             pltpu.VMEM((16, 128), BF16),
             pltpu.VMEM((rows, 128), BF16),
             pltpu.VMEM((rows, 128), F32),
-            pltpu.VMEM((head_devices, 2, 8, 128), F32),
-            pltpu.VMEM((head_devices, 2, 8, 128), F32),
+            pltpu.VMEM((2 * head_devices, 8, 128), BF16),
+            pltpu.VMEM((2 * head_devices, 8, 128), BF16),
             pltpu.VMEM((16, 128), F32),
-            pltpu.SemaphoreType.DMA((4,)),
-            pltpu.SemaphoreType.DMA((8,)),
-            pltpu.SemaphoreType.DMA((8,)),
+            pltpu.SemaphoreType.DMA((9,)),
+            pltpu.SemaphoreType.DMA((12,)),
+            pltpu.SemaphoreType.DMA((12,)),
+            pltpu.SemaphoreType.REGULAR((2,)),
         ],
         compiler_params=pltpu.CompilerParams(
-            collective_id=0, has_side_effects=True, vmem_limit_bytes=48 * 1024 * 1024
+            collective_id=0, has_side_effects=True, vmem_limit_bytes=62 * 1024 * 1024
         ),
         name="decode",
     )(

time: 52.6 us -> 46.5 us (0.88)
  local copies, waits for them, and re-layouts: 5.97 us -> 0.6 us
  Pallas kernels: 46.3 us -> 45.7 us
    unnamed x19 -> x1, local copies, waits for them, and re-layouts: 5.97 us -> 0.6 us
    pallas_call x1, Pallas kernels: 46.3 us -> 45.7 us  [shards(): pl.pallas_call(kernel, out_shape=pltpu.VMEM((out_rows, out_weight.shape[1...]
where the time goes in v2:
time: 46.5 us; the launch traced here: 46.3 us
  Pallas kernels  45.7 us (98%)
  local copies, waits for them, and re-layouts  0.6 us (1%)
    pallas_call x1, Pallas kernels, shards(): pl.pallas_call(kernel, out_shape=pltpu.VMEM((out_rows, out_weight.shape[1...  45.7 us

profile of v2, /device:TPU:1, one launch (start us, length us, event | category | flops | bytes accessed | tf_op | source)
XLA Modules:
  0.0 46.3 jit_solution(1555089159207912396)
XLA Ops:
  0.0 45.7 %decode.1 = bf16[16,128]{1,0:T(8,128)(2,1)S(1)} custom-call(bf16[2,1024]{1,0:T(2,128)(2,1)} %q_hbm.1, s32[1,64]{1,0:T(1,128)} %bitcast.3, s32[1,128]{1,0:T(1,128)} %bitcast.4, s32[1,64]{1,0:T(1,128)} %bitcast.5, s32[2]{0:T(128)} %suffix_len_hbm.1, bf16[2,512,128]{2,1,0:T(8,128)(2,1)} %global_hbm.1, bf16[2,2048,128]{2,1,0:T(8,128)(2,1)} %team_hbm.1, ...), custom_call_target="tpu_custom_call" | custom-call | tf_op jit(solution)/shard_map/decode/pallas_call | solution.py:347
  45.7 0.6 %copy.11 = bf16[16,128]{1,0:T(8,128)(2,1)} copy(bf16[16,128]{1,0:T(8,128)(2,1)S(1)} %decode.1) | data formatting | bytes 8192

commit v3 on v2

--- a/solution.py
+++ b/solution.py
@@ -35,6 +35,13 @@
     return dot(weights.astype(BF16), values), high, mass
 
 
+def fold(first, second):
+    top = jnp.maximum(first[1], second[1])
+    one, two = jnp.exp(first[1] - top), jnp.exp(second[1] - top)
+    total = one + two
+    return first[0] * (one / total) + second[0] * (two / total), top + jnp.log(total)
+
+
 def make_kernel(agent_devices, head_devices):
     chips = agent_devices // 2
     rows = chips * 16
@@ -46,7 +53,7 @@
         q_ref, lengths_ref, map_ref, owner_ref, suffix_len_ref, q_f32, q_own, q_all, global_kv, team_kv, suffix_kv, weight,
         part_out, part_in, lse_out, lse_in, att_own, att_all, att_f32,
         proj_out, proj_in, merged,
-        local_sem, send_sem, recv_sem, word,
+        local_sem, send_sem, recv_sem, word, above,
     ):
         a = lax.axis_index("agents")
         h = lax.axis_index("heads")
@@ -72,14 +79,27 @@
         heads = [(k, d) for k in range(head_devices) for d in range(2) if k or d]
 
         barrier = pltpu.get_barrier_semaphore()
-        greeted = line_peers + ring_peers + [sibling]
-        for peer in greeted:
+
+        def hello(peer):
             pl.semaphore_signal(barrier, inc=1, device_id=peer, device_id_type=MESH)
 
+        for peer in line_peers + [sibling]:
+            hello(peer)
+
+        @pl.when(z > 0)
+        def _():
+            hello(at(0, ring - 1))
+
+        for off in range(1, ring):
+            @pl.when(z + off < ring)
+            def _(off=off):
+                for k in range(lines):
+                    hello(at(k, off))
+
         @pl.when(z == 0)
         def _():
             for k in range(1, head_devices):
-                pl.semaphore_signal(barrier, inc=1, device_id=head_peer(k, 0), device_id_type=MESH)
+                hello(head_peer(k, 0))
 
         span = global_hbm.shape[1]
         own_span = pl.ds(pl.multiple_of(core * span, span), span)
@@ -107,13 +127,11 @@
                 ].astype(F32)
         q_own[...] = q_f32[...].astype(BF16)
 
-        @pl.when(z == 0)
-        def _():
-            pl.semaphore_wait(barrier, len(greeted) + head_devices - 1)
-
-        @pl.when(z != 0)
-        def _():
-            pl.semaphore_wait(barrier, len(greeted))
+        top_plane = (z + 1) // ring
+        bottom_plane = 1 - (z + ring - 1) // ring
+        pl.semaphore_wait(
+            barrier, lines * (z + 1) + 1 - top_plane + (head_devices - 1) * bottom_plane
+        )
 
         own_rows = pl.ds(pl.multiple_of(chip * 16, 16), 16)
         own_line = pl.ds(pl.multiple_of(y * 16, 16), 16)
@@ -137,15 +155,31 @@
         for peer in line_peers:
             send(q_own, q_all.at[own_line], 0, peer)
         keep(q_own, q_all.at[own_line], 0)
+
+        def landing_slot(slot):
+            return steps.index((ring - steps[slot]) % ring)
+
+        for slot in reversed(range(1, ring)):
+            off, there = steps[slot], landing_slot(slot)
+
+            @pl.when(z + off >= ring)
+            def _(off=off, there=there):
+                rows_there = pl.ds(pl.multiple_of(there * plane + y * 16, 16), 16)
+                for k in reversed(range(lines)):
+                    send(q_own, q_all.at[rows_there], 8 + there // 2, at(k, off))
+
+        @pl.when(z < ring - 1)
+        def _():
+            for off in range(1, ring):
+                @pl.when(z >= off)
+                def _(off=off):
+                    pl.semaphore_signal(
+                        above.at[z + 1], inc=1, device_id=at(0, ring - off), device_id_type=MESH
+                    )
+
         send(global_hbm, global_kv.at[:, own_span], 1, sibling)
         send(team_hbm, team_kv.at[core], 2, sibling)
         send(weight_hbm, weight.at[core], 3, sibling)
-
-        own_plane = q_all.at[pl.ds(0, plane)]
-        arrived(own_plane, 0)
-        for slot in reversed(range(1, ring)):
-            there = steps.index((ring - steps[slot]) % ring)
-            send(own_plane, q_all.at[pl.ds(there * plane, plane)], 8 + there // 2, at(0, steps[slot]))
 
         for copy in small[1:]:
             copy.wait()
@@ -185,6 +219,8 @@
             axis=0,
         )
         give = take.T
+        is_team = give > 0.5
+        give = give.astype(BF16)
         take = take.astype(BF16)
 
         local[2].wait()
@@ -201,6 +237,24 @@
             suffix_lse.append(high * scaling + jnp.log(mass))
         suffix_num = jnp.concatenate(suffix_num, axis=0)
         suffix_lse = jnp.concatenate(suffix_lse, axis=0)
+        others = rows // RING * 2 - plane
+        suffix_num = jnp.concatenate([suffix_num] * lines + [jnp.zeros((others, 128), F32)], axis=0)
+        suffix_lse = jnp.concatenate(
+            [jnp.where(y == j, suffix_lse, NEG) for j in range(lines)]
+            + [jnp.full((others, 1), NEG, F32)],
+            axis=0,
+        )
+
+        own_plane = q_all.at[pl.ds(0, plane)]
+        arrived(own_plane, 0)
+        for off in range(1, ring):
+            there = landing_slot(steps.index(off))
+
+            @pl.when(z + off < ring)
+            def _(off=off, there=there):
+                if off > 1:
+                    pl.semaphore_wait(above.at[z + off], 1)
+                send(own_plane, q_all.at[pl.ds(there * plane, plane)], 8 + there // 2, at(0, off))
 
         chunk = 2 * plane
         chunks = rows // chunk
@@ -211,108 +265,138 @@
             first = c * chunk + (plane if c == 0 else 0)
             arrived(q_all.at[pl.ds(first, (c + 1) * chunk - first)], 8 + c)
             scores = dot_t(q_all[pl.ds(c * chunk, chunk), :], global_kv[0])
-            prompt.append(softmax_part(scores, global_kv[1], scaling))
+            num, high, mass = softmax_part(scores, global_kv[1], scaling)
+            part = num / mass, high * scaling + jnp.log(mass)
+            if c == 0:
+                part = fold(part, (suffix_num, suffix_lse))
+            prompt.append(part)
+
+        @pl.when(z == 0)
+        def _():
+            for k in range(1, head_devices):
+                pl.semaphore_signal(word.at[0], inc=1, device_id=head_peer(k, 0), device_id_type=MESH)
 
         local[1].wait()
         arrived(team_hbm, 2)
         team_rows = dot(take, q_all[...]).astype(BF16)
-        team_num, team_high, team_mass = [], [], []
+        team_num, team_lse = [], []
         for slot in range(2):
             block = TEAM_CAP * 8
             scores = dot_t(team_rows[slot * block : slot * block + block], team_kv[slot, 0])
             scores = jnp.where(iota(scores.shape, 1) < spans[slot], scores, NEG)
             num, high, mass = softmax_part(scores, team_kv[slot, 1], scaling)
-            team_num.append(num)
-            team_high.append(high)
-            team_mass.append(mass)
+            team_num.append(num / mass)
+            team_lse.append(high * scaling + jnp.log(mass))
         team_num = jnp.concatenate(team_num, axis=0)
-        team_high = jnp.concatenate(team_high, axis=0)
-        team_mass = jnp.concatenate(team_mass, axis=0)
+        team_lse = jnp.concatenate(team_lse, axis=0)
         eye = iota((128, 128), 0) == iota((128, 128), 1)
-        high_lane = jnp.max(jnp.where(eye, team_high, NEG), axis=0, keepdims=True)
-        mass_lane = jnp.sum(jnp.where(eye, team_mass, 0.0), axis=0, keepdims=True)
+        lse_lane = jnp.max(jnp.where(eye, team_lse, NEG), axis=0, keepdims=True)
         coarse = team_num.astype(BF16)
-        fine = (team_num - coarse.astype(F32)).astype(BF16)
+        team_num = jnp.concatenate([coarse, (team_num - coarse.astype(F32)).astype(BF16)], axis=1)
 
         for c in range(chunks):
             span_rows = pl.ds(c * chunk, chunk)
-            num, high, mass = prompt[c]
-            chosen = give[c * chunk : c * chunk + chunk]
-            is_team = chosen > 0.5
-            t_high = jnp.max(jnp.where(is_team, high_lane, NEG), axis=-1, keepdims=True)
-            t_mass = jnp.sum(jnp.where(is_team, mass_lane, 0.0), axis=-1, keepdims=True)
-            chosen = chosen.astype(BF16)
-            t_num = dot(chosen, coarse) + dot(chosen, fine)
-            top = jnp.maximum(high, t_high)
-            g_factor = jnp.exp((high - top) * scaling)
-            t_factor = jnp.exp((t_high - top) * scaling)
-            mass = mass * g_factor + t_mass * t_factor
-            num = (num * g_factor + t_num * t_factor) / mass
+            num = dot(give[c * chunk : c * chunk + chunk], team_num)
+            lse = jnp.where(is_team[c * chunk : c * chunk + chunk], lse_lane, NEG)
+            lse = jnp.max(lse, axis=-1, keepdims=True)
+            num, lse = fold(prompt[c], (num[:, :128] + num[:, 128:], lse))
             part_out[span_rows, :] = num.astype(BF16)
             lse = jnp.where(
-                iota((chunk, 128), 1) == iota((chunk, 128), 0) % 16, top * scaling + jnp.log(mass), 0.0
+                iota((chunk, 128), 1) == iota((chunk, 128), 0) % 16, lse, 0.0
             )
             lse_out[pl.ds(c * chunk // 16, chunk // 16)] = jnp.sum(
                 lse.reshape(chunk // 16, 16, 128), axis=1, keepdims=True
             )
 
+        far_side = lax.rem(h, 2)
+
+        def block_of(line, at_ring):
+            middle = (line + 1) // 2 % 2
+            row_line = line // 2 * 2 + at_ring // 4
+            off = (at_ring % 4 + 4 * ((far_side + middle) % 2) - z + ring) % ring
+            some, back = (off + ring - 1) // ring, (off + ring // 2 - 1) // ring
+            slot = (1 - back) * (2 * off - some) + back * 2 * (ring - off)
+            return slot * lines + row_line
+
         for slot in reversed(range(ring)):
             for k in reversed(range(lines)):
                 if slot or k:
-                    block = slot * lines + lax.rem(y + k, lines)
+                    block = block_of(lax.rem(y + k, lines), lax.rem(z + steps[slot], ring))
                     peer = at(k, steps[slot])
                     send(part_out.at[pl.ds(pl.multiple_of(block * 16, 16), 16)], part_in.at[own_rows], 4, peer)
                     send(lse_out.at[block], lse_in.at[chip], 5, peer)
-        keep(part_out.at[own_line], part_in.at[own_rows], 4)
-        keep(lse_out.at[y], lse_in.at[chip], 5)
-
+        block = block_of(y, z)
+        keep(part_out.at[pl.ds(pl.multiple_of(block * 16, 16), 16)], part_in.at[own_rows], 4)
+        keep(lse_out.at[block], lse_in.at[chip], 5)
         arrived(lse_in, 5)
         lse = lse_in[...].reshape(chips, 128)
         lse = jnp.concatenate([lse, jnp.full((128 - chips, 128), NEG, F32)], axis=0).T[0:16]
-        top = jnp.maximum(jnp.max(lse, axis=-1, keepdims=True), suffix_lse)
-        factors = jnp.exp(lse - top)
-        suffix_factor = jnp.exp(suffix_lse - top)
-        total = jnp.sum(factors, axis=-1, keepdims=True) + suffix_factor
-        num = suffix_num * suffix_factor
+        factors = jnp.exp(lse - jnp.max(lse, axis=-1, keepdims=True))
+        factors = factors / jnp.sum(factors, axis=-1, keepdims=True)
         arrived(part_in, 4)
-        for j in range(chips):
+        num = part_in[pl.ds(0, 16), :].astype(F32) * factors[:, 0:1]
+        for j in range(1, chips):
             num = num + part_in[pl.ds(j * 16, 16), :].astype(F32) * factors[:, j : j + 1]
-        att_own[...] = (num / total).astype(BF16)
-
+        att_own[...] = num.astype(BF16)
+
+        kind = 12 + (y + 1) // 2 % 2
         for slot in reversed(range(ring)):
             for k in reversed(range(lines)):
                 if slot or k:
-                    send(att_own, att_all.at[own_rows], 6, at(k, steps[slot]))
-        keep(att_own, att_all.at[own_rows], 6)
+                    send(att_own, att_all.at[own_rows], kind, at(k, steps[slot]))
+        keep(att_own, att_all.at[own_rows], kind)
 
         @pl.when(z == 0)
         def _():
-            for k in range(1, head_devices):
-                pl.semaphore_signal(word.at[0], inc=1, device_id=head_peer(k, 0), device_id_type=MESH)
             pl.semaphore_wait(word.at[0], head_devices - 1)
             for peer in ring_peers:
                 pl.semaphore_signal(word.at[1], inc=1, device_id=peer, device_id_type=MESH)
 
         local[3].wait()
         arrived(weight_hbm, 3)
-        arrived(att_all, 6)
-        att_f32[...] = att_all[...].astype(F32)
-        att = jnp.concatenate(
-            [att_f32[pl.ds(j, rows // 8, stride=8), :] for j in range(8)], axis=1
-        ).astype(BF16)
-        for side in range(2):
-            proj_out[pl.ds(side * head_devices, head_devices)] = (
-                dot(att, weight[side]).astype(BF16).reshape(head_devices, 8, 128)
-            )
+
+        def project(spans, units):
+            parts = []
+            for start, size in spans:
+                att_f32[pl.ds(start, size), :] = att_all[pl.ds(start, size), :].astype(F32)
+            for j in range(8):
+                parts.append(
+                    jnp.concatenate(
+                        [att_f32[pl.ds(start + j, size // 8, stride=8), :] for start, size in spans], axis=0
+                    )
+                )
+            att = jnp.concatenate(parts, axis=1).astype(BF16)
+            for side in range(2):
+                sums = dot(att, weight[side]).astype(BF16).reshape(len(units), 8, 128)
+                for n, unit in enumerate(units):
+                    proj_out[side * head_devices + unit] = sums[n]
+
+        def to_heads(side_of, unit_of):
+            for k in range(head_devices // 2):
+                line = lax.rem(h // 2 + k, head_devices // 2)
+                there = line * 2 + side_of
+                for d in range(2):
+                    to_core = lax.rem(core + d, 2)
+                    src = proj_out.at[to_core * head_devices + unit_of(line)]
+                    yield k, d, src, (chip * 2 + to_core, there)
+
+        arrived(att_all.at[pl.ds(0, rows // 2)], 13)
+        project([(rows // 4, rows // 2)], [2, 3, 4, 5])
 
         @pl.when(z != 0)
         def _():
             pl.semaphore_wait(word.at[1], 1)
 
-        for k, d in heads:
-            to = (lax.rem(h + k, head_devices), lax.rem(core + d, 2))
-            send(proj_out.at[to[1] * head_devices + to[0]], proj_in.at[core * head_devices + h], 7, head_peer(k, d))
-        keep(proj_out.at[core * head_devices + h], proj_in.at[core * head_devices + h], 7)
+        landing = proj_in.at[core * head_devices + h]
+        for k, d, src, peer in to_heads(1 - far_side, lambda line: 2 + line):
+            send(src, landing, 7, peer)
+        arrived(att_all.at[pl.ds(0, rows // 2)], 12)
+        project([(0, rows // 4), (3 * rows // 4, rows // 4)], [0, 1, 6, 7])
+        for k, d, src, peer in to_heads(far_side, lambda line: line // 2 * 6 + line % 2):
+            if k or d:
+                send(src, landing, 7, peer)
+            else:
+                keep(src, landing, 7)
         arrived(proj_in, 7)
         for side in range(2):
             summed = jnp.sum(proj_in[pl.ds(side * head_devices, head_devices)].astype(F32), axis=0)
@@ -330,7 +414,7 @@
         sent(weight_hbm, 3)
         sent(part_in.at[others], 4)
         sent(lse_in.at[pl.ds(0, chips - 1)], 5)
-        sent(att_all.at[others], 6)
+        sent(att_all.at[others], kind)
         sent(proj_in.at[pl.ds(0, len(heads))], 7)
 
     return kernel, rows, chips
@@ -373,9 +457,10 @@
             pltpu.VMEM((2 * head_devices, 8, 128), BF16),
             pltpu.VMEM((16, 128), F32),
             pltpu.SemaphoreType.DMA((9,)),
-            pltpu.SemaphoreType.DMA((12,)),
-            pltpu.SemaphoreType.DMA((12,)),
+            pltpu.SemaphoreType.DMA((14,)),
+            pltpu.SemaphoreType.DMA((14,)),
             pltpu.SemaphoreType.REGULAR((2,)),
+            pltpu.SemaphoreType.REGULAR((RING,)),
         ],
         compiler_params=pltpu.CompilerParams(
             collective_id=0, has_side_effects=True, vmem_limit_bytes=62 * 1024 * 1024

time: 46.5 us -> 43 us (0.925)
  Pallas kernels: 45.7 us -> 42.3 us
    pallas_call x1, Pallas kernels: 45.7 us -> 42.3 us  [shards(): pl.pallas_call(kernel, out_shape=pltpu.VMEM((out_rows, out_weight.shape[1...]
where the time goes in v3:
time: 43 us; the launch traced here: 42.9 us
  Pallas kernels  42.3 us (98%)
  local copies, waits for them, and re-layouts  0.6 us (1%)
    pallas_call x1, Pallas kernels, shards(): pl.pallas_call(kernel, out_shape=pltpu.VMEM((out_rows, out_weight.shape[1...  42.3 us

profile of v3, /device:TPU:1, one launch (start us, length us, event | category | flops | bytes accessed | tf_op | source)
XLA Modules:
  0.0 42.9 jit_solution(1013032244234944818)
XLA Ops:
  0.0 42.3 %decode.1 = bf16[16,128]{1,0:T(8,128)(2,1)S(1)} custom-call(bf16[2,1024]{1,0:T(2,128)(2,1)} %q_hbm.1, s32[1,64]{1,0:T(1,128)} %bitcast.3, s32[1,128]{1,0:T(1,128)} %bitcast.4, s32[1,64]{1,0:T(1,128)} %bitcast.5, s32[2]{0:T(128)} %suffix_len_hbm.1, bf16[2,512,128]{2,1,0:T(8,128)(2,1)} %global_hbm.1, bf16[2,2048,128]{2,1,0:T(8,128)(2,1)} %team_hbm.1, ...), custom_call_target="tpu_custom_call" | custom-call | tf_op jit(solution)/shard_map/decode/pallas_call | solution.py:431
  42.3 0.6 %copy.11 = bf16[16,128]{1,0:T(8,128)(2,1)} copy(bf16[16,128]{1,0:T(8,128)(2,1)S(1)} %decode.1) | data formatting | bytes 8192

commit v4 on v3

--- a/solution.py
+++ b/solution.py
@@ -11,6 +11,7 @@
 TEAM_CAP = 8
 RING = 8
 NEG = -1e30
+LOG2E = math.log2(math.e)
 MESH = pl.DeviceIdType.MESH
 F32 = jnp.float32
 BF16 = jnp.bfloat16
@@ -30,7 +31,7 @@
 
 def softmax_part(scores, values, scaling):
     high = jnp.max(scores, axis=-1, keepdims=True)
-    weights = jnp.exp((scores - high) * scaling)
+    weights = jnp.exp2((scores - high) * (scaling * LOG2E))
     mass = jnp.sum(weights, axis=-1, keepdims=True)
     return dot(weights.astype(BF16), values), high, mass
 
@@ -197,11 +198,12 @@
         spread = (iota((agents, rows), 0) == row_agent).astype(BF16)
         owner = owner_ref[...]
         team_ids = iota(owner.shape, 1)
-        picks, spans = [], []
+        picks, hidden = [], []
         for slot in range(2):
             here = owner == chip * 2 + slot
             team = jnp.sum(jnp.where(here, team_ids, 0), axis=1, keepdims=True)
-            spans.append(jnp.sum(jnp.where(here, lengths_ref[...], 0), axis=1, keepdims=True))
+            length = jnp.sum(jnp.where(here, lengths_ref[...], 0), axis=1, keepdims=True)
+            hidden.append(jnp.where(iota((1, team_hbm.shape[1]), 1) < length, 0.0, NEG))
             member = jnp.logical_and(team_of == team, mine)
             members = jnp.broadcast_to(jnp.where(member, 1.0, 0.0), (8, agents)).astype(BF16)
             rank = dot(members, before)[0:1]
@@ -266,7 +268,7 @@
             arrived(q_all.at[pl.ds(first, (c + 1) * chunk - first)], 8 + c)
             scores = dot_t(q_all[pl.ds(c * chunk, chunk), :], global_kv[0])
             num, high, mass = softmax_part(scores, global_kv[1], scaling)
-            part = num / mass, high * scaling + jnp.log(mass)
+            part = num * (1.0 / mass), high * scaling + jnp.log(mass)
             if c == 0:
                 part = fold(part, (suffix_num, suffix_lse))
             prompt.append(part)
@@ -283,9 +285,9 @@
         for slot in range(2):
             block = TEAM_CAP * 8
             scores = dot_t(team_rows[slot * block : slot * block + block], team_kv[slot, 0])
-            scores = jnp.where(iota(scores.shape, 1) < spans[slot], scores, NEG)
+            scores = scores + hidden[slot]
             num, high, mass = softmax_part(scores, team_kv[slot, 1], scaling)
-            team_num.append(num / mass)
+            team_num.append(num * (1.0 / mass))
             team_lse.append(high * scaling + jnp.log(mass))
         team_num = jnp.concatenate(team_num, axis=0)
         team_lse = jnp.concatenate(team_lse, axis=0)
@@ -372,11 +374,11 @@
                     proj_out[side * head_devices + unit] = sums[n]
 
         def to_heads(side_of, unit_of):
-            for k in range(head_devices // 2):
-                line = lax.rem(h // 2 + k, head_devices // 2)
-                there = line * 2 + side_of
-                for d in range(2):
-                    to_core = lax.rem(core + d, 2)
+            for d in (1, 0):
+                to_core = lax.rem(core + d, 2)
+                for k in (2, 1, 3, 0):
+                    line = lax.rem(h // 2 + k, head_devices // 2)
+                    there = line * 2 + side_of
                     src = proj_out.at[to_core * head_devices + unit_of(line)]
                     yield k, d, src, (chip * 2 + to_core, there)
 

time: 43 us -> 42.6 us (level)
  no operation moved by 1% of the time
where the time goes in v4:
time: 42.6 us; the launch traced here: 42.5 us
  Pallas kernels  41.9 us (98%)
  local copies, waits for them, and re-layouts  0.6 us (1%)
    pallas_call x1, Pallas kernels, shards(): pl.pallas_call(kernel, out_shape=pltpu.VMEM((out_rows, out_weight.shape[1...  41.9 us

profile of v4, /device:TPU:1, one launch (start us, length us, event | category | flops | bytes accessed | tf_op | source)
XLA Modules:
  0.0 42.5 jit_solution(6212327056161105929)
XLA Ops:
  0.0 41.9 %decode.1 = bf16[16,128]{1,0:T(8,128)(2,1)S(1)} custom-call(bf16[2,1024]{1,0:T(2,128)(2,1)} %q_hbm.1, s32[1,64]{1,0:T(1,128)} %bitcast.3, s32[1,128]{1,0:T(1,128)} %bitcast.4, s32[1,64]{1,0:T(1,128)} %bitcast.5, s32[2]{0:T(128)} %suffix_len_hbm.1, bf16[2,512,128]{2,1,0:T(8,128)(2,1)} %global_hbm.1, bf16[2,2048,128]{2,1,0:T(8,128)(2,1)} %team_hbm.1, ...), custom_call_target="tpu_custom_call" | custom-call | tf_op jit(solution)/shard_map/decode/pallas_call | solution.py:433
  41.9 0.6 %copy.11 = bf16[16,128]{1,0:T(8,128)(2,1)} copy(bf16[16,128]{1,0:T(8,128)(2,1)S(1)} %decode.1) | data formatting | bytes 8192

commit v5 on v4

--- a/solution.py
+++ b/solution.py
@@ -311,6 +311,14 @@
             )
 
         far_side = lax.rem(h, 2)
+        upper = y // 2
+        hops = [min(step, ring - step) for step in steps]
+        order = sorted(((s, t) for s in range(ring) for t in range(lines)), key=lambda p: p[1] - hops[p[0]])
+
+        def line_of(slot, t):
+            if slot == 0:
+                return lax.rem(y + lines - 1 - t, lines)
+            return (1 - upper) * (lines - 1 - t) + upper * t
 
         def block_of(line, at_ring):
             middle = (line + 1) // 2 % 2
@@ -320,11 +328,11 @@
             slot = (1 - back) * (2 * off - some) + back * 2 * (ring - off)
             return slot * lines + row_line
 
-        for slot in reversed(range(ring)):
-            for k in reversed(range(lines)):
-                if slot or k:
-                    block = block_of(lax.rem(y + k, lines), lax.rem(z + steps[slot], ring))
-                    peer = at(k, steps[slot])
+        for slot, t in order:
+                if slot or t < lines - 1:
+                    to_line = line_of(slot, t)
+                    block = block_of(to_line, lax.rem(z + steps[slot], ring))
+                    peer = at(to_line - y + lines, steps[slot])
                     send(part_out.at[pl.ds(pl.multiple_of(block * 16, 16), 16)], part_in.at[own_rows], 4, peer)
                     send(lse_out.at[block], lse_in.at[chip], 5, peer)
         block = block_of(y, z)
@@ -342,10 +350,9 @@
         att_own[...] = num.astype(BF16)
 
         kind = 12 + (y + 1) // 2 % 2
-        for slot in reversed(range(ring)):
-            for k in reversed(range(lines)):
-                if slot or k:
-                    send(att_own, att_all.at[own_rows], kind, at(k, steps[slot]))
+        for slot, t in order:
+            if slot or t < lines - 1:
+                send(att_own, att_all.at[own_rows], kind, at(line_of(slot, t) - y + lines, steps[slot]))
         keep(att_own, att_all.at[own_rows], kind)
 
         @pl.when(z == 0)

time: 42.6 us -> 42.9 us (level)
  no operation moved by 1% of the time
where the time goes in v5:
time: 42.9 us; the launch traced here: 42.7 us
  Pallas kernels  42.1 us (98%)
  local copies, waits for them, and re-layouts  0.6 us (1%)
    pallas_call x1, Pallas kernels, shards(): pl.pallas_call(kernel, out_shape=pltpu.VMEM((out_rows, out_weight.shape[1...  42.1 us

profile of v5, /device:TPU:1, one launch (start us, length us, event | category | flops | bytes accessed | tf_op | source)
XLA Modules:
  0.0 42.7 jit_solution(14538548082751584796)
XLA Ops:
  0.0 42.1 %decode.1 = bf16[16,128]{1,0:T(8,128)(2,1)S(1)} custom-call(bf16[2,1024]{1,0:T(2,128)(2,1)} %q_hbm.1, s32[1,64]{1,0:T(1,128)} %bitcast.3, s32[1,128]{1,0:T(1,128)} %bitcast.4, s32[1,64]{1,0:T(1,128)} %bitcast.5, s32[2]{0:T(128)} %suffix_len_hbm.1, bf16[2,512,128]{2,1,0:T(8,128)(2,1)} %global_hbm.1, bf16[2,2048,128]{2,1,0:T(8,128)(2,1)} %team_hbm.1, ...), custom_call_target="tpu_custom_call" | custom-call | tf_op jit(solution)/shard_map/decode/pallas_call | solution.py:440
  42.1 0.6 %copy.11 = bf16[16,128]{1,0:T(8,128)(2,1)} copy(bf16[16,128]{1,0:T(8,128)(2,1)S(1)} %decode.1) | data formatting | bytes 8192
